TPU v7x, 256 devices: a whole 4x4x8 slice. The times are simulated.
256 devices in a mesh: snap: 16 (over z, core), vtx: 16 (over y, x).
Axes of the slice: x: 4, y: 4, z: 8, core: 2. Of those that a mesh axis runs over, the one named last changes fastest.
Arguments:
- feats: float32 [16, 16384, 512], P('snap', 'vtx'), may hold values from -6 to 6
- col_ids: int32 [16, 128, 16], P('snap', 'vtx'), may hold values from 0 to 127
- tiles: float32 [16, 128, 16, 128, 128], P('snap', 'vtx'), may hold values from -0.125 to 0.125
- w_first: float32 [512, 256], replicated, may hold values from -0.25 to 0.25
- w_input: float32 [256, 1024], replicated, may hold values from -0.375 to 0.375
- w_recur: float32 [256, 1024], replicated, may hold values from -0.375 to 0.375
- lstm_bias: float32 [1024], replicated, may hold values from -3 to 3
- w_second: float32 [256, 256], replicated, may hold values from -0.375 to 0.375
Outputs:
- output: float32 [16, 16384, 256], P('snap', 'vtx')
Inputs may be any that keep to these rules, and one draw needn't show every extreme that they name: `col_ids`: every entry names a row block of the same snapshot's graph; a few blocks are named far more often than others.
All inputs are finite; a program needn't handle non-finite values.
Results may differ from a plain program's by a relative error of at most 0.0003.
Values sent between devices are 32-bit elements; how exact they have to be, the bound alone decides.
A program may use at most 128 MiB of HBM per device.

v0:
```python
import jax
import jax.numpy as jnp
from jax import lax
from jax.sharding import PartitionSpec as P


def block_sum(tile_set, column_ids, source):
    tile_edge = tile_set.shape[-1]
    width = source.shape[-1]
    blocks = source.reshape(source.shape[0] // tile_edge, tile_edge, width)

    def row_block(operands):
        tiles_here, ids_here = operands
        picked = blocks[ids_here]
        return jnp.einsum("ktu,kuw->tw", tiles_here, picked, precision=lax.Precision.HIGHEST)

    summed = lax.map(row_block, (tile_set, column_ids))
    return summed.reshape(-1, width)


def row_scale(tiles):
    sums = jnp.sum(tiles * tiles, axis=(2, 4))
    return lax.rsqrt(1.0 + sums).reshape(tiles.shape[0], -1)[..., None]


def recurrence(pre_time, w_recur, lstm_bias):
    hidden_size = w_recur.shape[0]

    def advance(carry, pre_step):
        state_h, state_c = carry
        gates = pre_step + jnp.dot(state_h, w_recur, precision=lax.Precision.HIGHEST) + lstm_bias
        gate_i = gates[:, :hidden_size]
        gate_f = gates[:, hidden_size : 2 * hidden_size]
        gate_g = gates[:, 2 * hidden_size : 3 * hidden_size]
        gate_o = gates[:, 3 * hidden_size :]
        state_c = jax.nn.sigmoid(gate_f) * state_c + jax.nn.sigmoid(gate_i) * jnp.tanh(gate_g)
        state_h = jax.nn.sigmoid(gate_o) * jnp.tanh(state_c)
        return ((state_h, state_c), state_h)

    zeros = jnp.zeros((pre_time.shape[1], hidden_size), jnp.float32)
    _, states = lax.scan(advance, (zeros, zeros), pre_time)
    return states


def on_device(feats, col_ids, tiles, w_first, w_input, w_recur, lstm_bias, w_second):
    scale = row_scale(tiles)
    whole = lax.all_gather(feats, "vtx", axis=1, tiled=True)
    mixed = scale * (feats + jax.vmap(block_sum)(tiles, col_ids, whole))
    hidden_one = jax.nn.relu(
        jnp.einsum("svf,fh->svh", mixed, w_first, precision=lax.Precision.HIGHEST)
    )
    timelines = lax.all_to_all(hidden_one, "snap", split_axis=1, concat_axis=0, tiled=True)
    pre_time = jnp.einsum("svh,hg->svg", timelines, w_input, precision=lax.Precision.HIGHEST)
    states = recurrence(pre_time, w_recur, lstm_bias)
    returned = lax.all_to_all(states, "snap", split_axis=0, concat_axis=1, tiled=True)
    whole_two = lax.all_gather(returned, "vtx", axis=1, tiled=True)
    mixed_two = scale * (returned + jax.vmap(block_sum)(tiles, col_ids, whole_two))
    return jnp.einsum("svh,hg->svg", mixed_two, w_second, precision=lax.Precision.HIGHEST)


def solution(mesh):
    placed = (
        P("snap", "vtx", None),
        P("snap", "vtx", None),
        P("snap", "vtx", None, None, None),
        P(),
        P(),
        P(),
        P(),
        P(),
    )
    return jax.shard_map(
        on_device, mesh=mesh, in_specs=placed, out_specs=P("snap", "vtx", None), check_vma=False
    )
```

profile of v0, /device:TPU:1, one launch (start us, length us, event | category | flops | bytes accessed | tf_op | source)
XLA Modules:
  0.0 618.2 jit_solution(13330983946178340313)
XLA Ops:
  6.5 0.7 all-gather.3.cloned.1.call-update
  7.3 4.0 multiply_reduce_fusion
  11.3 204.4 %all-gather.3.cloned.1.call-done = f32[1,16384,512]{2,1,0:T(8,128)} async-done(((f32[1,1024,512]{2,1,0:T(8,128)}), f32[1,16384,512]{2,1,0:T(8,128)}) %all-gather.3.cloned.1.call-update) | async-done | bytes 33554448 | tf_op jit(solution)/shard_map/all_gather | solution.py:47
  215.7 91.9 %while.35 = (s32[]{:T(128)}, f32[8,1,128,512]{3,2,1,0:T(8,128)}, f32[8,1,16,128,128]{4,3,2,1,0:T(8,128)}, s32[8,1,16]{2,1,0:T(1,128)}, f32[1,128,128,512]{3,2,1,0:T(8,128)}, /*index=5*/s32[]{:T(128)}) while((s32[]{:T(128)}, f32[8,1,128,512]{3,2,1,0:T(8,128)}, f32[8,1,16,128,128]{4,3,2,1,0:T(8,128)}, s32[8,1,16]{2,1,0:T(1,128)}, ...), condition=%wide.region_2.3_spmd, body=%wide.region_1.2_spmd.sunk | while | flops 1610612864 | bytes 13895369 | solution.py:17
  215.7 0.8 compare_select_fusion.4
  216.5 5.2 gather_fusion
  221.7 5.7 fusion.62
  228.0 5.0 gather_fusion
  233.1 5.7 fusion.62
  239.4 5.0 gather_fusion
  244.4 5.7 fusion.62
  250.7 5.0 gather_fusion
  255.8 5.7 fusion.62
  262.1 5.5 gather_fusion
  267.6 5.6 fusion.62
  273.9 5.1 gather_fusion
  279.0 5.6 fusion.62
  285.3 5.1 gather_fusion
  290.4 5.6 fusion.62
  296.7 5.2 gather_fusion
  302.0 5.7 fusion.62
  307.6 3.5 fusion.35
  311.2 2.0 copy.12
  313.2 7.4 %all-to-all-start = ((f32[1,1024,256]{2,0,1:T(1,128)}), f32[1,1024,256]{2,0,1:T(1,128)S(1)}, u32[]{:S(2)}, u32[]{:S(2)}) async-start(f32[1,1024,256]{2,0,1:T(1,128)} %copy.12), calls=%async_computation | async-start | bytes 2097152 | tf_op jit(solution)/shard_map/all_to_all | solution.py:52
  320.7 27.9 %all-to-all-done = f32[1,1024,256]{2,0,1:T(1,128)S(1)} async-done(((f32[1,1024,256]{2,0,1:T(1,128)}), f32[1,1024,256]{2,0,1:T(1,128)S(1)}, u32[]{:S(2)}, u32[]{:S(2)}) %all-to-all-start) | async-done | bytes 1048608 | tf_op jit(solution)/shard_map/all_to_all | solution.py:52
  348.7 5.0 fusion.39
  353.7 29.0 %while.37 = (s32[]{:T(128)}, f32[64,256]{1,0:T(8,128)S(1)}, f32[64,256]{1,0:T(8,128)S(1)}, f32[16,64,256]{2,1,0:T(8,128)S(1)}, f32[16,64,1024]{2,1,0:T(8,128)}, ...) while((s32[]{:T(128)}, f32[64,256]{1,0:T(8,128)S(1)}, ...), condition=%wide.region_4.5_spmd.clone, body=%wide.region_3.4_spmd.clone.sunk | while | flops 201703424 | bytes 2166896 | solution.py:41
  353.7 1.7 fusion.68
  355.5 1.7 fusion.68
  357.3 1.7 fusion.68
  359.1 1.7 fusion.68
  360.9 1.7 fusion.68
  362.8 1.7 fusion.68
  364.6 1.7 fusion.68
  366.4 1.7 fusion.68
  368.2 1.7 fusion.68
  370.0 1.7 fusion.68
  371.8 1.7 fusion.68
  373.6 1.7 fusion.68
  375.5 1.7 fusion.68
  377.3 1.7 fusion.68
  379.1 1.7 fusion.68
  380.9 1.7 fusion.68
  382.7 32.0 %all_to_all.27 = f32[16,64,256]{2,1,0:T(8,128)} all-to-all(f32[16,64,256]{2,1,0:T(8,128)S(1)} %get-tuple-element.97), channel_id=1, replica_groups=mesh['snap'=16,'vtx'=16] {'snap'}, dimensions={0} | all-to-all | bytes 2097152 | tf_op jit(solution)/shard_map/all_to_all | solution.py:55
  414.7 111.7 %all-gather.5.cloned.1.call-done = f32[1,16384,256]{2,1,0:T(8,128)} async-done(((f32[1,1024,256]{2,1,0:T(8,128)}), f32[1,16384,256]{2,1,0:T(8,128)}) %all-gather.5.cloned.1.call-update) | async-done | bytes 16777232 | tf_op jit(solution)/shard_map/all_gather | solution.py:56
  526.4 81.2 %while.36 = (s32[]{:T(128)}, f32[8,1,128,256]{3,2,1,0:T(8,128)}, f32[8,1,16,128,128]{4,3,2,1,0:T(8,128)}, s32[8,1,16]{2,1,0:T(1,128)}, f32[1,128,128,256]{3,2,1,0:T(8,128)}, /*index=5*/s32[]{:T(128)}) while((s32[]{:T(128)}, f32[8,1,128,256]{3,2,1,0:T(8,128)}, f32[8,1,16,128,128]{4,3,2,1,0:T(8,128)}, s32[8,1,16]{2,1,0:T(1,128)}, ...), condition=%wide.region_6.7_spmd, body=%wide.region_5.6_spmd.sunk | while | flops 805306496 | bytes 7472841 | solution.py:17
  527.1 6.4 %gather_fusion.1 = f32[16,128,256]{2,1,0:T(8,128)S(1)} fusion(f32[1,128,128,256]{3,2,1,0:T(8,128)} %get-tuple-element.352, s32[16]{0:T(128)S(1)} %or_bitcast_fusion.5), kind=kCustom, calls=%fused_computation.1.clone.1 | custom fusion | bytes 4194432 | tf_op jit(solution)/shard_map/vmap()/while/body/eval_jaxpr/gather | solution.py:14
  533.5 3.0 fusion.65
  537.2 6.4 %gather_fusion.1 = f32[16,128,256]{2,1,0:T(8,128)S(1)} fusion(f32[1,128,128,256]{3,2,1,0:T(8,128)} %get-tuple-element.352, s32[16]{0:T(128)S(1)} %or_bitcast_fusion.5), kind=kCustom, calls=%fused_computation.1.clone.1 | custom fusion | bytes 4194432 | tf_op jit(solution)/shard_map/vmap()/while/body/eval_jaxpr/gather | solution.py:14
  543.7 3.0 fusion.65
  547.4 6.4 %gather_fusion.1 = f32[16,128,256]{2,1,0:T(8,128)S(1)} fusion(f32[1,128,128,256]{3,2,1,0:T(8,128)} %get-tuple-element.352, s32[16]{0:T(128)S(1)} %or_bitcast_fusion.5), kind=kCustom, calls=%fused_computation.1.clone.1 | custom fusion | bytes 4194432 | tf_op jit(solution)/shard_map/vmap()/while/body/eval_jaxpr/gather | solution.py:14
  553.8 3.0 fusion.65
  557.5 6.4 %gather_fusion.1 = f32[16,128,256]{2,1,0:T(8,128)S(1)} fusion(f32[1,128,128,256]{3,2,1,0:T(8,128)} %get-tuple-element.352, s32[16]{0:T(128)S(1)} %or_bitcast_fusion.5), kind=kCustom, calls=%fused_computation.1.clone.1 | custom fusion | bytes 4194432 | tf_op jit(solution)/shard_map/vmap()/while/body/eval_jaxpr/gather | solution.py:14
  564.0 3.0 fusion.65
  567.7 6.4 %gather_fusion.1 = f32[16,128,256]{2,1,0:T(8,128)S(1)} fusion(f32[1,128,128,256]{3,2,1,0:T(8,128)} %get-tuple-element.352, s32[16]{0:T(128)S(1)} %or_bitcast_fusion.5), kind=kCustom, calls=%fused_computation.1.clone.1 | custom fusion | bytes 4194432 | tf_op jit(solution)/shard_map/vmap()/while/body/eval_jaxpr/gather | solution.py:14
  574.1 3.0 fusion.65
  577.8 6.4 %gather_fusion.1 = f32[16,128,256]{2,1,0:T(8,128)S(1)} fusion(f32[1,128,128,256]{3,2,1,0:T(8,128)} %get-tuple-element.352, s32[16]{0:T(128)S(1)} %or_bitcast_fusion.5), kind=kCustom, calls=%fused_computation.1.clone.1 | custom fusion | bytes 4194432 | tf_op jit(solution)/shard_map/vmap()/while/body/eval_jaxpr/gather | solution.py:14
  584.3 3.0 fusion.65
  588.0 6.4 %gather_fusion.1 = f32[16,128,256]{2,1,0:T(8,128)S(1)} fusion(f32[1,128,128,256]{3,2,1,0:T(8,128)} %get-tuple-element.352, s32[16]{0:T(128)S(1)} %or_bitcast_fusion.5), kind=kCustom, calls=%fused_computation.1.clone.1 | custom fusion | bytes 4194432 | tf_op jit(solution)/shard_map/vmap()/while/body/eval_jaxpr/gather | solution.py:14
  594.4 3.0 fusion.65
  598.1 6.4 %gather_fusion.1 = f32[16,128,256]{2,1,0:T(8,128)S(1)} fusion(f32[1,128,128,256]{3,2,1,0:T(8,128)} %get-tuple-element.352, s32[16]{0:T(128)S(1)} %or_bitcast_fusion.5), kind=kCustom, calls=%fused_computation.1.clone.1 | custom fusion | bytes 4194432 | tf_op jit(solution)/shard_map/vmap()/while/body/eval_jaxpr/gather | solution.py:14
  604.6 3.0 fusion.65
  607.6 1.8 fusion.38
  609.4 2.0 convolution_bitcast_fusion.2
  (83 shorter events, 11.7 us)
Async XLA Ops:
  6.5 342.1 %copy-start = (f32[256,1024]{1,0:T(8,128)S(1)}, f32[256,1024]{1,0:T(8,128)}, u32[]{:S(2)}) copy-start(f32[256,1024]{1,0:T(8,128)} %param.18) | copy-start | bytes 3145732
  6.5 209.2 %all-gather.3.cloned.1.call-start = ((), (), s32[]{:S(2)}) async-start(), calls=%async_computation.2 | async-start | bytes 35651584 | tf_op jit(solution)/shard_map/all_gather | solution.py:47
  215.7 91.9 %copy-start.2 = (f32[1,1024,512]{2,1,0:T(8,128)S(1)}, f32[1,1024,512]{2,1,0:T(8,128)}, u32[]{:S(2)}) copy-start(f32[1,1024,512]{2,1,0:T(8,128)} %param.14) | copy-start | bytes 6291460
  313.2 35.3 %all-to-all-start = ((f32[1,1024,256]{2,0,1:T(1,128)}), f32[1,1024,256]{2,0,1:T(1,128)S(1)}, u32[]{:S(2)}, u32[]{:S(2)}) async-start(f32[1,1024,256]{2,0,1:T(1,128)} %copy.12), calls=%async_computation | async-start | bytes 2097152 | tf_op jit(solution)/shard_map/all_to_all | solution.py:52
  320.6 205.8 %all-gather.5.cloned.1.call-start = ((), (), s32[]{:S(2)}) async-start(), calls=%async_computation.3 | async-start | bytes 17825792 | tf_op jit(solution)/shard_map/all_gather | solution.py:56
  348.6 5.0 copy-start.1
  348.6 5.0 copy-start.4
  607.6 1.8 copy-start.3
Sparse Core Ops, SparseCore 0:
  9.8 205.8 all-gather.2
  414.9 111.5 all-gather.4
where the time goes:
time: 620 us; the launch traced here: 618 us
  waiting for transfers between devices  345 us (56%)
  matrix products  107 us (17%)
  local copies, waits for them, and re-layouts  95 us (15%)
  blocking collectives  32 us (5%)
  other arithmetic  18 us (3%)
  between operations  13.5 us (2%)
  starting transfers between devices  7.44 us (1%)
    all_gather x1, waiting for transfers between devices, on_device(): whole = lax.all_gather(feats, 'vtx', axis=1, tiled=True)  204 us
    all_gather x1, waiting for transfers between devices, on_device(): whole_two = lax.all_gather(returned, 'vtx', axis=1, tiled=True)  112 us
    gather x32, local copies, waits for them, and re-layouts, row_block(): picked = blocks[ids_here]  92.9 us
    dot_general x16, matrix products, row_block(): jnp.einsum('ktu,kuw->tw', tiles_here, picked, precision=lax.Precision.HIG...  69.3 us
    all_to_all x1, blocking collectives, on_device(): lax.all_to_all(states, 'snap', split_axis=0, concat_axis=1, tiled=True)  32 us
    all_to_all x1, waiting for transfers between devices, on_device(): lax.all_to_all(hidden_one, 'snap', split_axis=1, concat_axis=0, tiled=True)  27.9 us
    dot_general x16, matrix products, advance(): jnp.dot(state_h, w_recur, precision=lax.Precision.HIGHEST)  27.3 us
  transfers between devices with their start and end apart: 3, of which 3 were waited for; matrix products, arithmetic and copies ran while one was open for 1% of the time, Pallas kernels for 0%

commit v1 on v0

v1 whole, which is shorter than its diff:
```python
import jax
import jax.numpy as jnp
from jax import lax
from jax.experimental import pallas as pl
from jax.experimental.pallas import tpu as pltpu
from jax.sharding import PartitionSpec as P

BF16, F32 = jnp.bfloat16, jnp.float32


def halves(x):
    high = x.astype(BF16)
    return high, (x - high.astype(F32)).astype(BF16)


def dot(a, b):
    return jnp.dot(a, b, preferred_element_type=F32)


def dot3(a, b_high, b_low):
    a_high, a_low = halves(a)
    return dot(a_high, b_high) + (dot(a_low, b_high) + dot(a_high, b_low))


def conv_kernel(first, ids_ref, tiles_ref, own_ref, whole_ref, out_ref, th, tl, yh, yl):
    row = pl.program_id(0)
    kt, edge = tiles_ref.shape[1], tiles_ref.shape[2]
    squares = jnp.zeros((edge, edge), F32)
    for k in range(kt):
        at = slice(k * edge, (k + 1) * edge)
        tile = tiles_ref[0, k]
        squares += tile * tile
        th[:, at], tl[:, at] = halves(tile)
        yh[at, :], yl[at, :] = halves(whole_ref[ids_ref[row, k]])
    scale = lax.rsqrt(1.0 + jnp.sum(squares, axis=1, keepdims=True))
    total = dot(th[...], yh[...]) + (dot(tl[...], yh[...]) + dot(th[...], yl[...]))
    total = scale * (own_ref[...] + total)
    out_ref[...] = jnp.maximum(total, 0.0) if first else total


def conv(first, tiles, ids, own, whole):
    blocks, kt, edge, _ = tiles.shape
    width = own.shape[-1]
    return pl.pallas_call(
        lambda *refs: conv_kernel(first, *refs),
        grid=(blocks,),
        in_specs=[
            pl.BlockSpec(memory_space=pltpu.SMEM),
            pl.BlockSpec((1, kt, edge, edge), lambda r: (r, 0, 0, 0)),
            pl.BlockSpec((edge, width), lambda r: (r, 0)),
            pl.BlockSpec(memory_space=pltpu.VMEM),
        ],
        out_specs=pl.BlockSpec((edge, width), lambda r: (r, 0)),
        out_shape=jax.ShapeDtypeStruct(own.shape, F32),
        scratch_shapes=[
            pltpu.VMEM((edge, kt * edge), BF16),
            pltpu.VMEM((edge, kt * edge), BF16),
            pltpu.VMEM((kt * edge, width), BF16),
            pltpu.VMEM((kt * edge, width), BF16),
        ],
        compiler_params=pltpu.CompilerParams(vmem_limit_bytes=44 << 20),
    )(ids, tiles, own, whole)


def sigmoid(x):
    return 0.5 * jnp.tanh(0.5 * x) + 0.5


def lstm_kernel(x_ref, w_in_ref, w_rec_ref, bias_ref, w_two_ref, out_ref, pre, wh, wl, rh, rl):
    steps, rows, hidden = x_ref.shape
    wh[...], wl[...] = halves(w_in_ref[...])
    rh[...], rl[...] = halves(w_rec_ref[...])

    def fill(s, _):
        pre[s] = dot3(x_ref[s], wh[...], wl[...]) + bias_ref[...]
        return 0

    lax.fori_loop(0, steps, fill, 0)

    def advance(s, carry):
        h, c = carry
        gates = pre[s] + dot3(h, rh[...], rl[...])
        i, f, g, o = (gates[:, q * hidden : (q + 1) * hidden] for q in range(4))
        c = sigmoid(f) * c + sigmoid(i) * jnp.tanh(g)
        h = sigmoid(o) * jnp.tanh(c)
        out_ref[s] = h
        return h, c

    zeros = jnp.zeros((rows, hidden), F32)
    lax.fori_loop(0, steps, advance, (zeros, zeros))
    two_high, two_low = halves(w_two_ref[...])
    states = out_ref[...].reshape(steps * rows, hidden)
    out_ref[...] = dot3(states, two_high, two_low).reshape(steps, rows, hidden)


def lstm(x, w_input, w_recur, bias, w_second):
    steps, rows, hidden = x.shape
    return pl.pallas_call(
        lstm_kernel,
        in_specs=[pl.BlockSpec(memory_space=pltpu.VMEM)] * 5,
        out_specs=pl.BlockSpec(memory_space=pltpu.VMEM),
        out_shape=jax.ShapeDtypeStruct(x.shape, F32),
        scratch_shapes=[
            pltpu.VMEM((steps, rows, 4 * hidden), F32),
            pltpu.VMEM((hidden, 4 * hidden), BF16),
            pltpu.VMEM((hidden, 4 * hidden), BF16),
            pltpu.VMEM((hidden, 4 * hidden), BF16),
            pltpu.VMEM((hidden, 4 * hidden), BF16),
        ],
        compiler_params=pltpu.CompilerParams(vmem_limit_bytes=40 << 20),
    )(x, w_input, w_recur, bias.reshape(1, -1), w_second)


def on_device(feats, col_ids, tiles, w_first, w_input, w_recur, lstm_bias, w_second):
    feats, ids, tiles = feats[0], col_ids[0], tiles[0]
    edge, hidden = tiles.shape[-1], w_second.shape[0]
    y = jnp.dot(feats, w_first, precision=lax.Precision.HIGH)
    whole = lax.all_gather(y, "vtx", axis=0, tiled=True).reshape(-1, edge, hidden)
    hidden_one = conv(True, tiles, ids, y, whole)
    timelines = lax.all_to_all(hidden_one[None], "snap", split_axis=1, concat_axis=0, tiled=True)
    states = lstm(timelines, w_input, w_recur, lstm_bias, w_second)
    z = lax.all_to_all(states, "snap", split_axis=0, concat_axis=1, tiled=True)[0]
    whole = lax.all_gather(z, "vtx", axis=0, tiled=True).reshape(-1, edge, hidden)
    return conv(False, tiles, ids, z, whole)[None]


def solution(mesh):
    placed = (
        P("snap", "vtx", None),
        P("snap", "vtx", None),
        P("snap", "vtx", None, None, None),
        P(),
        P(),
        P(),
        P(),
        P(),
    )
    return jax.shard_map(
        on_device, mesh=mesh, in_specs=placed, out_specs=P("snap", "vtx", None), check_vma=False
    )
```

time: 620 us -> 366 us (0.59)
  waiting for transfers between devices: 345 us -> 232 us
  matrix products: 107 us -> 3.01 us
  local copies, waits for them, and re-layouts: 95 us -> 8.59 us
  Pallas kernels: 0 us -> 41.1 us
  blocking collectives: 32 us -> 67.5 us
  other arithmetic: 18 us -> 0 us
  starting transfers between devices: 7.44 us -> 0.04 us
    dot_general x35 -> x1, matrix products: 107 us -> 3.01 us  [on_device(): y = jnp.dot(feats, w_first, precision=lax.Precision.HIGH)]
    gather x32 -> x0, local copies, waits for them, and re-layouts: 92.9 us -> none  [row_block(): picked = blocks[ids_here]]
    all_gather x2, waiting for transfers between devices: 316 us -> 232 us  [the longest x1 120 us: on_device(): lax.all_gather(y, 'vtx', axis=0, tiled=True).reshape(-1, edge, hidden)]
    pallas_call x0 -> x3, Pallas kernels: none -> 41.1 us  [the longest x2 27.3 us: conv(): pl.pallas_call(lambda *refs: conv_kernel(first, *refs), grid=(blocks,), i...]
    all_to_all x1 -> x2, blocking collectives: 32 us -> 67.5 us  [the longest x1 36.2 us: on_device(): lax.all_to_all(hidden_one[None], 'snap', split_axis=1, concat_axis=0, til...]
    all_to_all x1 -> x0, waiting for transfers between devices: 27.9 us -> none  [on_device(): lax.all_to_all(hidden_one, 'snap', split_axis=1, concat_axis=0, tiled=True)]
    select_n x16 -> x0, other arithmetic: 10.7 us -> none  [row_block(): picked = blocks[ids_here]]
    unnamed x11 -> x19, local copies, waits for them, and re-layouts: 0.09 us -> 7.51 us
  transfers between devices with their start and end apart: 3 -> 2, of which waited for: 3 -> 2; matrix products, arithmetic and copies ran while one was open for 1% -> 0% of each run, Pallas kernels for 0% -> 0%
where the time goes in v1:
time: 366 us; the launch traced here: 365 us
  waiting for transfers between devices  232 us (63%)
  blocking collectives  67.5 us (18%)
  Pallas kernels  41.1 us (11%)
  between operations  13.5 us (4%)
  local copies, waits for them, and re-layouts  8.59 us (2%)
    all_gather x1, waiting for transfers between devices, on_device(): lax.all_gather(y, 'vtx', axis=0, tiled=True).reshape(-1, edge, hidden)  120 us
    all_gather x1, waiting for transfers between devices, on_device(): lax.all_gather(z, 'vtx', axis=0, tiled=True).reshape(-1, edge, hidden)  111 us
    all_to_all x1, blocking collectives, on_device(): lax.all_to_all(hidden_one[None], 'snap', split_axis=1, concat_axis=0, til...  36.2 us
    all_to_all x1, blocking collectives, on_device(): lax.all_to_all(states, 'snap', split_axis=0, concat_axis=1, tiled=True)[0]  31.3 us
    pallas_call x2, Pallas kernels, conv(): pl.pallas_call(lambda *refs: conv_kernel(first, *refs), grid=(blocks,), i...  27.3 us
    pallas_call x1, Pallas kernels, lstm(): pl.pallas_call(lstm_kernel, in_specs=[pl.BlockSpec(memory_space=pltpu.VME...  13.7 us
    unnamed x19, local copies, waits for them, and re-layouts  7.51 us
  transfers between devices with their start and end apart: 2, of which 2 were waited for; matrix products, arithmetic and copies ran while one was open for 0% of the time, Pallas kernels for 0%

profile of v1, /device:TPU:1, one launch (start us, length us, event | category | flops | bytes accessed | tf_op | source)
XLA Modules:
  0.0 365.4 jit_solution(13115491265908592890)
XLA Ops:
  6.5 0.0 copy-start
  6.5 0.0 copy-start.7
  6.5 0.0 all-gather.3.cloned.1.call-start
  6.5 1.6 copy-done
  8.1 3.0 fusion.refs_2_
  11.1 0.0 all-gather.3.cloned.1.call-update
  11.2 0.0 all-gather.5.cloned.1.call-start
  11.2 120.2 %all-gather.3.cloned.1.call-done = f32[16384,256]{1,0:T(8,128)} async-done(((f32[1024,256]{1,0:T(8,128)}), f32[16384,256]{1,0:T(8,128)}) %all-gather.3.cloned.1.call-update) | async-done | bytes 16777232 | tf_op jit(solution)/shard_map/all_gather | solution.py:118
  131.4 0.0 copy-done.7
  131.4 0.0 copy-start.2
  131.4 1.2 copy-done.2
  132.6 14.0 %shard_map.82 = f32[1024,256]{1,0:T(8,128)S(1)} custom-call(s32[8,16]{1,0:T(8,128)S(1)} %bitcast.19, f32[8,16,128,128]{3,2,1,0:T(8,128)} %bitcast.13, f32[1024,256]{1,0:T(8,128)S(1)} %copy-done.2, f32[128,128,256]{2,1,0:T(8,128)} %bitcast.22), custom_call_target="tpu_custom_call" | custom-call | tf_op jit(solution)/shard_map/pallas_call | solution.py:44
  146.6 1.1 copy.9
  147.7 0.0 copy-start.4
  147.7 0.0 copy-start.5
  147.7 0.0 copy-start.6
  147.8 0.0 copy-start.8
  147.8 36.2 %all_to_all.21 = f32[1,1024,256]{2,0,1:T(1,128)S(1)} all-to-all(f32[1,1024,256]{2,0,1:T(1,128)S(1)} %copy.9), channel_id=1, replica_groups=mesh['snap'=16,'vtx'=16] {'snap'}, dimensions={1} | all-to-all | bytes 2097152 | tf_op jit(solution)/shard_map/all_to_all | solution.py:120
  184.0 0.1 copy.10
  184.1 0.0 copy-done.4
  184.1 0.0 copy-done.5
  184.1 0.0 copy-done.6
  184.1 0.0 copy-done.8
  184.1 13.7 %shard_map.83 = f32[16,64,256]{2,1,0:T(8,128)S(1)} custom-call(f32[16,64,256]{2,1,0:T(8,128)S(1)} %bitcast.18, f32[256,1024]{1,0:T(8,128)S(1)} %copy-done.4, f32[256,1024]{1,0:T(8,128)S(1)} %copy-done.5, f32[1,1024]{1,0:T(1,128)S(1)} %bitcast.21, f32[256,256]{1,0:T(8,128)S(1)} %copy-done.6), custom_call_target="tpu_custom_call" | custom-call | tf_op jit(solution)/shard_map/pallas_call | solution.py:98
  197.8 31.3 %all_to_all.22 = f32[16,64,256]{2,1,0:T(8,128)} all-to-all(f32[16,64,256]{2,1,0:T(8,128)S(1)} %shard_map.83), channel_id=1, replica_groups=mesh['snap'=16,'vtx'=16] {'snap'}, dimensions={0} | all-to-all | bytes 2097152 | tf_op jit(solution)/shard_map/all_to_all | solution.py:122
  229.1 0.0 all-gather.5.cloned.1.call-update
  229.2 111.5 %all-gather.5.cloned.1.call-done = f32[16384,256]{1,0:T(8,128)} async-done(((f32[1024,256]{1,0:T(8,128)}), f32[16384,256]{1,0:T(8,128)}) %all-gather.5.cloned.1.call-update) | async-done | bytes 16777232 | tf_op jit(solution)/shard_map/all_gather | solution.py:123
  340.6 0.0 copy-start.1
  340.6 3.4 copy-done.1
  344.0 0.0 copy-start.3
  344.0 1.2 copy-done.3
  345.2 13.4 %shard_map.84 = f32[1024,256]{1,0:T(8,128)} custom-call(s32[8,16]{1,0:T(8,128)S(1)} %bitcast.20, f32[8,16,128,128]{3,2,1,0:T(8,128)S(1)} %bitcast.14, f32[1024,256]{1,0:T(8,128)S(1)} %bitcast.16, f32[128,128,256]{2,1,0:T(8,128)} %bitcast.23), custom_call_target="tpu_custom_call" | custom-call | tf_op jit(solution)/shard_map/pallas_call | solution.py:44
Async XLA Ops:
  6.5 1.6 copy-start
  6.5 124.9 %copy-start.7 = (s32[1,8,16]{2,1,0:T(8,128)S(1)}, s32[1,8,16]{2,1,0:T(8,128)}, u32[]{:S(2)}) copy-start(s32[1,8,16]{2,1,0:T(8,128)} %param.9) | copy-start | bytes 1540
  6.5 124.9 %all-gather.3.cloned.1.call-start = ((), (), s32[]{:S(2)}) async-start(), calls=%async_computation.2 | async-start | bytes 17825792 | tf_op jit(solution)/shard_map/all_gather | solution.py:118
  11.2 329.5 %all-gather.5.cloned.1.call-start = ((), (), s32[]{:S(2)}) async-start(), calls=%async_computation.3 | async-start | bytes 17825792 | tf_op jit(solution)/shard_map/all_gather | solution.py:123
  131.4 1.2 copy-start.2
  147.7 36.3 %copy-start.4 = (f32[256,1024]{1,0:T(8,128)S(1)}, f32[256,1024]{1,0:T(8,128)}, u32[]{:S(2)}) copy-start(f32[256,1024]{1,0:T(8,128)} %w_in_ref.1) | copy-start | bytes 3145732
  147.7 36.3 %copy-start.5 = (f32[256,1024]{1,0:T(8,128)S(1)}, f32[256,1024]{1,0:T(8,128)}, u32[]{:S(2)}) copy-start(f32[256,1024]{1,0:T(8,128)} %w_rec_ref.1) | copy-start | bytes 3145732
  147.7 36.3 %copy-start.6 = (f32[256,256]{1,0:T(8,128)S(1)}, f32[256,256]{1,0:T(8,128)}, u32[]{:S(2)}) copy-start(f32[256,256]{1,0:T(8,128)} %w_two_ref.1) | copy-start | bytes 786436
  147.8 36.3 %copy-start.8 = (f32[1024]{0:T(1024)S(1)}, f32[1024]{0:T(1024)}, u32[]{:S(2)}) copy-start(f32[1024]{0:T(1024)} %param.14) | copy-start | bytes 12292
  340.6 3.4 copy-start.1
  344.0 1.2 copy-start.3
Sparse Core Ops, SparseCore 0:
  11.3 120.0 all-gather.2
  229.3 111.3 all-gather.4

commit v2 on v0

v2 whole, which is shorter than its diff:
```python
import jax
import jax.numpy as jnp
from jax import lax
from jax.experimental import pallas as pl
from jax.experimental.pallas import tpu as pltpu
from jax.sharding import PartitionSpec as P

BF16, F32 = jnp.bfloat16, jnp.float32
MESH = pl.DeviceIdType.MESH
SIDE = 4
SNAPS = 16
EDGE = 128
LANES = 128
KT = 16
BLOCKS = 8
BATCH = 32
HIDDEN = 256
GATHER_SEMS = 40


def halves(x):
    high = x.astype(BF16)
    return high, (x - high.astype(F32)).astype(BF16)


def dot(a, b):
    return jnp.dot(a, b, preferred_element_type=F32)


def dot3(a, b_high, b_low):
    a_high, a_low = halves(a)
    return dot(a_high, b_high) + (dot(a_low, b_high) + dot(a_high, b_low))


def sigmoid(x):
    return 0.5 * jnp.tanh(0.5 * x) + 0.5


class Gather:
    def __init__(self, buffer, source, first, count, send_sem, recv_sem, base):
        self.buffer, self.source, self.first, self.count = buffer, source, first, count
        self.send_sem, self.recv_sem, self.base = send_sem, recv_sem, base
        me = lax.axis_index("vtx")
        self.x, self.y = lax.rem(me, SIDE), lax.div(me, SIDE)
        self.me = me
        self.started = []

    def device(self, half, da, db):
        dx, dy = (da, db) if half == 0 else (db, da)
        return lax.rem(self.y + (dy + SIDE), SIDE) * SIDE + lax.rem(self.x + (dx + SIDE), SIDE)

    def rows(self, half, part):
        size = self.count // 2
        start = half * size
        if part is not None:
            size //= 2
            start += part * size
        return start, size

    def place(self, half, da, db, part):
        start, size = self.rows(half, part)
        return self.buffer.at[pl.ds(self.device(half, da, db) * BLOCKS + (self.first + start), size)]

    def number(self, half, da, db, part):
        along = {-1: 0, 1: 1, 2: 2}
        if db == 0:
            number = along[da]
            number += part or 0
        else:
            number = 4 + 4 * (0, -1, 1, 2).index(da) + along[db] + (part or 0)
        return self.base + half * 20 + number

    def copy(self, half, axis, way, da, db, part):
        seen = lambda d: 2 if d in (-1, 1) and d == -way else -way
        if axis == 0:
            to, number = self.device(half, way, 0), self.number(half, seen(da), db, part)
        else:
            to, number = self.device(half, 0, way), self.number(half, da, seen(db), part)
        place = self.place(half, da, db, part)
        source = place
        if da == 0 and db == 0 and self.source is not None:
            start, size = self.rows(half, part)
            source = self.source.at[pl.ds(self.first + start, size)]
        return pltpu.make_async_remote_copy(
            src_ref=source,
            dst_ref=place,
            send_sem=self.send_sem.at[number],
            recv_sem=self.recv_sem.at[number],
            device_id={"vtx": to},
            device_id_type=MESH,
        )

    def send(self, half, axis, way, da, db, part=None):
        copy = self.copy(half, axis, way, da, db, part)
        copy.start()
        self.started.append(copy)

    def wait(self, half, da, db, part=None):
        number = self.number(half, da, db, part)
        place = self.place(half, da, db, part)
        pltpu.make_async_remote_copy(
            src_ref=place,
            dst_ref=place,
            send_sem=self.send_sem.at[number],
            recv_sem=self.recv_sem.at[number],
            device_id={"vtx": self.device(half, 1, 0)},
            device_id_type=MESH,
        ).wait_recv()

    def both(self, half, da):
        for way in (1, -1):
            self.send(half, 1, way, da, 0)

    def own(self):
        for half in (0, 1):
            for way in (1, -1):
                self.send(half, 0, way, 0, 0)
        for half in (0, 1):
            self.both(half, 0)

    def ring(self):
        for half in (0, 1):
            self.wait(half, -1, 0)
            self.send(half, 0, 1, -1, 0, 0)
            self.wait(half, 1, 0)
            self.send(half, 0, -1, 1, 0, 1)
        for half in (0, 1):
            self.both(half, -1)
            self.both(half, 1)

    def onward(self, da):
        for half in (0, 1):
            self.wait(half, da, -1)
            self.send(half, 1, 1, da, -1, 0)
            self.wait(half, da, 1)
            self.send(half, 1, -1, da, 1, 1)

    def opposite(self):
        for half in (0, 1):
            self.wait(half, 2, 0, 0)
            self.wait(half, 2, 0, 1)
            self.both(half, 2)

    def last(self):
        for da in (0, -1, 1, 2):
            for half in (0, 1):
                for part in (0, 1):
                    self.wait(half, da, 2, part)

    def wait_sent(self):
        for copy in self.started:
            copy.wait_send()


def kernel(
    ids_ref, feats_ref, w_first_ref, bias_ref, tiles_hbm, w_in_hbm, w_rec_hbm, w_two_hbm, out_ref,
    buf0, buf1, staged, tcat, scales, ycat, hid, xin, pre, zout, zin,
    w_in, w_rec, w_two, in_high, in_low, rec_high, rec_low,
    g_send, g_recv, x_send, x_recv, z_send, z_recv, local_sem, tile_sem, weight_sem, free_sem,
):
    snap, me = lax.axis_index("snap"), lax.axis_index("vtx")
    x, y = lax.rem(me, SIDE), lax.div(me, SIDE)
    bufs = (buf0, buf1)
    others = [lax.rem(snap + k, SNAPS) for k in range(1, SNAPS)]
    beside = [
        lax.rem(y + dy, SIDE) * SIDE + lax.rem(x + dx, SIDE)
        for dx, dy in ((1, 0), (SIDE - 1, 0), (0, 1), (0, SIDE - 1))
    ]

    weights = [
        pltpu.make_async_copy(a, b, weight_sem.at[i])
        for i, (a, b) in enumerate(((w_in_hbm, w_in), (w_rec_hbm, w_rec), (w_two_hbm, w_two)))
    ]

    def tile_copy(r):
        return pltpu.make_async_copy(tiles_hbm.at[r], staged.at[r], tile_sem.at[r])

    barrier = pltpu.get_barrier_semaphore()
    for device in beside:
        pl.semaphore_signal(barrier, inc=1, device_id={"vtx": device}, device_id_type=MESH)
    for device in others:
        pl.semaphore_signal(barrier, inc=1, device_id={"snap": device}, device_id_type=MESH)

    for r in range(BLOCKS):
        tile_copy(r).start()
    for copy in weights:
        copy.start()

    def first_product(c):
        high, low = halves(w_first_ref[:, c * LANES : (c + 1) * LANES])

        def some(i, _):
            part = dot3(feats_ref[pl.ds(i * 256, 256), :], high, low)
            bufs[c][me * BLOCKS + 2 * i] = part[:EDGE]
            bufs[c][me * BLOCKS + 2 * i + 1] = part[EDGE:]
            return 0

        lax.fori_loop(0, BLOCKS // 2, some, 0)

    first_product(0)
    pl.semaphore_wait(barrier, len(beside) + len(others))

    one = [Gather(bufs[c], None, 0, BLOCKS, g_send, g_recv, c * GATHER_SEMS) for c in (0, 1)]
    one[0].own()
    first_product(1)

    def split_tiles(start, stop):
        def block(r, _):
            tile_copy(r).wait()
            squares = jnp.zeros((EDGE, EDGE), F32)
            for k in range(KT):
                tile = staged[r, k]
                squares += tile * tile
                high, low = halves(tile)
                tcat[r, :EDGE, k * EDGE : (k + 1) * EDGE] = high
                tcat[r, EDGE:, k * EDGE : (k + 1) * EDGE] = low
            scale = lax.rsqrt(1.0 + jnp.sum(squares, axis=1, keepdims=True))
            scales[r] = jnp.broadcast_to(scale, (EDGE, LANES))
            return 0

        lax.fori_loop(start, stop, block, 0)

    def conv(c, start, stop, first):
        def block(r, _):
            for k in range(KT):
                high, low = halves(bufs[c][ids_ref[r, k]])
                ycat[k * EDGE : (k + 1) * EDGE, :LANES] = high
                ycat[k * EDGE : (k + 1) * EDGE, LANES:] = low
            out = dot(tcat[r], ycat[...])
            total = (out[:EDGE, :LANES] + out[:EDGE, LANES:]) + (out[EDGE:, :LANES] + out[EDGE:, LANES:])
            total = scales[r] * (bufs[c][me * BLOCKS + r] + total)
            if first:
                hid[c, r] = jnp.maximum(total, 0.0)
            else:
                out_ref[pl.ds(pl.multiple_of(r * EDGE, EDGE), EDGE), c * LANES : (c + 1) * LANES] = total
            return 0

        lax.fori_loop(start, stop, block, 0)

    def shares(ref, c, b, j):
        rows = pl.ds(pl.multiple_of(lax.rem(j, 4) * BATCH, BATCH), BATCH)
        return ref.at[c, 4 * b + lax.div(j, 4), rows]

    x_sent = []

    def x_copy(c, b, k):
        to = others[k - 1]
        return pltpu.make_async_remote_copy(
            src_ref=shares(hid, c, b, to),
            dst_ref=xin.at[c, b, snap],
            send_sem=x_send.at[c, b, k],
            recv_sem=x_recv.at[c, b, k],
            device_id={"snap": to},
            device_id_type=MESH,
        )

    def x_local(c, b):
        return pltpu.make_async_copy(shares(hid, c, b, snap), xin.at[c, b, snap], x_send.at[c, b, 0])

    def x_start(c, b):
        for k in range(1, SNAPS):
            copy = x_copy(c, b, k)
            copy.start()
            x_sent.append(copy)
        x_local(c, b).start()

    def x_wait(c, b):
        x_local(c, b).wait()
        for k in range(1, SNAPS):
            source = lax.rem(snap + (SNAPS - k), SNAPS)
            pltpu.make_async_remote_copy(
                src_ref=xin.at[c, b, source],
                dst_ref=xin.at[c, b, source],
                send_sem=x_send.at[c, b, k],
                recv_sem=x_recv.at[c, b, k],
                device_id={"snap": source},
                device_id_type=MESH,
            ).wait_recv()

    def input_product(c, b):
        deep = slice(c * LANES, (c + 1) * LANES)

        def some(i, _):
            rows = pl.ds(pl.multiple_of(i * EDGE, EDGE), EDGE)
            part = dot3(xin[c, b, pl.ds(i * 4, 4)].reshape(EDGE, LANES), in_high[deep, :], in_low[deep, :])
            pre[b, rows] = part + (bias_ref[...] if c == 0 else pre[b, rows])
            return 0

        lax.fori_loop(0, SNAPS * BATCH // EDGE, some, 0)

    def z_copy(b, s):
        return pltpu.make_async_remote_copy(
            src_ref=zout.at[b, s],
            dst_ref=shares(zin, slice(None), b, snap),
            send_sem=z_send.at[b, s],
            recv_sem=z_recv.at[b, snap],
            device_id={"snap": s},
            device_id_type=MESH,
        )

    def z_local(b):
        return pltpu.make_async_copy(zout.at[b, snap], shares(zin, slice(None), b, snap), local_sem.at[b])

    def z_start(b, s, z):
        zout[b, s, 0] = z[:, :LANES]
        zout[b, s, 1] = z[:, LANES:]

        @pl.when(s != snap)
        def _():
            z_copy(b, s).start()

        @pl.when(s == snap)
        def _():
            z_local(b).start()

    def z_wait(b):
        z_local(b).wait()
        for source in others:
            pltpu.make_async_remote_copy(
                src_ref=shares(zin, slice(None), b, source),
                dst_ref=shares(zin, slice(None), b, source),
                send_sem=z_send.at[b, source],
                recv_sem=z_recv.at[b, source],
                device_id={"snap": source},
                device_id_type=MESH,
            ).wait_recv()
        for c in (0, 1):
            for i in range(4 * b, 4 * b + 4):
                bufs[c][me * BLOCKS + i] = zin[c, i]

    def cell(gates, state_c):
        i, f, g, o = (gates[:, q * HIDDEN : (q + 1) * HIDDEN] for q in range(4))
        state_c = sigmoid(f) * state_c + sigmoid(i) * jnp.tanh(g)
        return sigmoid(o) * jnp.tanh(state_c), state_c

    def begin(b):
        return cell(pre[b, :BATCH], jnp.zeros((BATCH, HIDDEN), F32))

    def product(h):
        high, low = halves(h)
        both = dot(jnp.concatenate([high, low], axis=0), rec_high[...])
        return both[:BATCH] + (both[BATCH:] + dot(high, rec_low[...]))

    def steps(b, start, stop, carry):
        def advance(s, carry):
            h, state_c = carry
            wide = product(h)
            rows = pl.ds(pl.multiple_of(s * BATCH, BATCH), BATCH)
            new = cell(pre[b, rows] + wide[:, : 4 * HIDDEN], state_c)
            z_start(b, s - 1, wide[:, 4 * HIDDEN :])
            return new

        return lax.fori_loop(start, stop, advance, carry)

    def finish(b, carry):
        last = slice(4 * HIDDEN, 5 * HIDDEN)
        z_start(b, SNAPS - 1, dot3(carry[0], rec_high[:, last], rec_low[:, last]))

    split_tiles(0, 4)
    one[0].ring()
    split_tiles(4, 8)
    for copy in weights:
        copy.wait()
    in_high[...], in_low[...] = halves(w_in[...])
    rec_high[:, : 4 * HIDDEN], rec_low[:, : 4 * HIDDEN] = halves(w_rec[...])
    rec_high[:, 4 * HIDDEN :], rec_low[:, 4 * HIDDEN :] = halves(w_two[...])
    one[0].onward(0)
    one[0].opposite()
    one[0].onward(-1)
    one[0].onward(1)
    one[1].own()
    one[0].onward(2)
    one[0].last()

    conv(0, 0, 4, True)
    x_start(0, 0)
    one[1].ring()
    conv(0, 4, 8, True)
    x_start(0, 1)
    one[1].onward(0)
    one[1].opposite()
    x_wait(0, 0)
    x_wait(0, 1)
    input_product(0, 0)
    one[1].onward(-1)
    one[1].onward(1)
    input_product(0, 1)
    one[1].onward(2)
    one[1].last()

    conv(1, 0, 4, True)
    x_start(1, 0)
    conv(1, 4, 8, True)
    x_start(1, 1)
    one[0].wait_sent()
    one[1].wait_sent()
    for device in beside:
        pl.semaphore_signal(free_sem, inc=1, device_id={"vtx": device}, device_id_type=MESH)

    x_wait(1, 0)
    input_product(1, 0)
    finish(0, steps(0, 1, SNAPS, begin(0)))
    x_wait(1, 1)
    input_product(1, 1)
    carry = steps(1, 1, 8, begin(1))
    z_wait(0)
    pl.semaphore_wait(free_sem, len(beside))
    two = [
        [
            Gather(bufs[c], zin.at[c], 4 * b, 4, g_send, g_recv, (2 + 2 * b + c) * GATHER_SEMS)
            for c in (0, 1)
        ]
        for b in (0, 1)
    ]
    two[0][0].own()
    two[0][1].own()
    finish(1, steps(1, 8, SNAPS, carry))
    two[0][0].ring()
    two[0][1].ring()
    z_wait(1)
    two[1][0].own()
    two[0][0].onward(0)
    two[0][0].opposite()
    two[0][1].onward(0)
    two[0][1].opposite()
    for da in (-1, 1, 2):
        two[0][0].onward(da)
    two[1][1].own()
    two[1][0].ring()
    for da in (-1, 1, 2):
        two[0][1].onward(da)
    two[1][0].onward(0)
    two[1][0].opposite()
    two[1][1].ring()
    for da in (-1, 1, 2):
        two[1][0].onward(da)
    two[0][0].last()
    two[0][1].last()
    two[1][0].last()
    conv(0, 0, 2, False)
    two[1][1].onward(0)
    two[1][1].opposite()
    conv(0, 2, 4, False)
    two[1][1].onward(-1)
    two[1][1].onward(1)
    conv(0, 4, 8, False)
    two[1][1].onward(2)
    two[1][1].last()
    conv(1, 0, 8, False)

    for b in (0, 1):
        for c in (0, 1):
            two[b][c].wait_sent()
    for copy in x_sent:
        copy.wait_send()
    for b in (0, 1):
        for device in others:
            z_copy(b, device).wait_send()


def on_device(feats, col_ids, tiles, w_first, w_input, w_recur, lstm_bias, w_second):
    rows = BLOCKS * EDGE
    whole = (lax.axis_size("vtx") * BLOCKS, EDGE, LANES)
    vmem, hbm = pl.BlockSpec(memory_space=pltpu.VMEM), pl.BlockSpec(memory_space=pl.ANY)
    dma = pltpu.SemaphoreType.DMA
    out = pl.pallas_call(
        kernel,
        in_specs=[pl.BlockSpec(memory_space=pltpu.SMEM), vmem, vmem, vmem, hbm, hbm, hbm, hbm],
        out_specs=vmem,
        out_shape=jax.ShapeDtypeStruct((rows, HIDDEN), F32),
        scratch_shapes=[
            pltpu.VMEM(whole, F32),
            pltpu.VMEM(whole, F32),
            pltpu.VMEM((BLOCKS, KT, EDGE, EDGE), F32),
            pltpu.VMEM((BLOCKS, 2 * EDGE, KT * EDGE), BF16),
            pltpu.VMEM((BLOCKS, EDGE, LANES), F32),
            pltpu.VMEM((KT * EDGE, 2 * LANES), BF16),
            pltpu.VMEM((2, BLOCKS, EDGE, LANES), F32),
            pltpu.VMEM((2, 2, SNAPS, BATCH, LANES), F32),
            pltpu.VMEM((2, SNAPS * BATCH, 4 * HIDDEN), F32),
            pltpu.VMEM((2, SNAPS, 2, BATCH, LANES), F32),
            pltpu.VMEM((2, BLOCKS, EDGE, LANES), F32),
            pltpu.VMEM((HIDDEN, 4 * HIDDEN), F32),
            pltpu.VMEM((HIDDEN, 4 * HIDDEN), F32),
            pltpu.VMEM((HIDDEN, HIDDEN), F32),
            pltpu.VMEM((HIDDEN, 4 * HIDDEN), BF16),
            pltpu.VMEM((HIDDEN, 4 * HIDDEN), BF16),
            pltpu.VMEM((HIDDEN, 5 * HIDDEN), BF16),
            pltpu.VMEM((HIDDEN, 5 * HIDDEN), BF16),
            dma((6 * GATHER_SEMS,)),
            dma((6 * GATHER_SEMS,)),
            dma((2, 2, SNAPS)),
            dma((2, 2, SNAPS)),
            dma((2, SNAPS)),
            dma((2, SNAPS)),
            dma((2,)),
            dma((BLOCKS,)),
            dma((3,)),
            pltpu.SemaphoreType.REGULAR,
        ],
        compiler_params=pltpu.CompilerParams(
            collective_id=0, has_side_effects=True, vmem_limit_bytes=58 << 20
        ),
    )(
        col_ids[0], feats[0], w_first, lstm_bias.reshape(1, -1), tiles[0], w_input, w_recur, w_second
    )
    return out[None]


def solution(mesh):
    placed = (
        P("snap", "vtx", None),
        P("snap", "vtx", None),
        P("snap", "vtx", None, None, None),
        P(),
        P(),
        P(),
        P(),
        P(),
    )
    return jax.shard_map(
        on_device, mesh=mesh, in_specs=placed, out_specs=P("snap", "vtx", None), check_vma=False
    )
```

time: 620 us -> 233 us (0.38)
  waiting for transfers between devices: 345 us -> 0 us
  Pallas kernels: 0 us -> 228 us
  matrix products: 107 us -> 0 us
  local copies, waits for them, and re-layouts: 95 us -> 2.26 us
  blocking collectives: 32 us -> 0 us
  other arithmetic: 18 us -> 0 us
  between operations: 13.5 us -> 0.01 us
  starting transfers between devices: 7.44 us -> 0 us
    all_gather x2 -> x0, waiting for transfers between devices: 316 us -> none  [the longest x1 204 us: on_device(): whole = lax.all_gather(feats, 'vtx', axis=1, tiled=True)]
    pallas_call x0 -> x1, Pallas kernels: none -> 228 us  [on_device(): pl.pallas_call(kernel, in_specs=[pl.BlockSpec(memory_space=pltpu.SMEM), v...]
    dot_general x35 -> x0, matrix products: 107 us -> none  [the longest x16 69.3 us: row_block(): jnp.einsum('ktu,kuw->tw', tiles_here, picked, precision=lax.Precision.HIG...]
    gather x32 -> x0, local copies, waits for them, and re-layouts: 92.9 us -> none  [row_block(): picked = blocks[ids_here]]
    all_to_all x1 -> x0, blocking collectives: 32 us -> none  [on_device(): lax.all_to_all(states, 'snap', split_axis=0, concat_axis=1, tiled=True)]
    all_to_all x1 -> x0, waiting for transfers between devices: 27.9 us -> none  [on_device(): lax.all_to_all(hidden_one, 'snap', split_axis=1, concat_axis=0, tiled=True)]
    select_n x16 -> x0, other arithmetic: 10.7 us -> none  [row_block(): picked = blocks[ids_here]]
    all_to_all x1 -> x0, starting transfers between devices: 7.4 us -> none  [on_device(): lax.all_to_all(hidden_one, 'snap', split_axis=1, concat_axis=0, tiled=True)]
  transfers between devices with their start and end apart: 3 -> 0, of which waited for: 3 -> 0; matrix products, arithmetic and copies ran while one was open for 1% -> 0% of each run, Pallas kernels for 0% -> 0%
where the time goes in v2:
time: 233 us; the launch traced here: 230 us
  Pallas kernels  228 us (98%)
    pallas_call x1, Pallas kernels, on_device(): pl.pallas_call(kernel, in_specs=[pl.BlockSpec(memory_space=pltpu.SMEM), v...  228 us

profile of v2, /device:TPU:1, one launch (start us, length us, event | category | flops | bytes accessed | tf_op | source)
XLA Modules:
  0.0 229.9 jit_solution(15363548165858340673)
XLA Ops:
  0.0 227.6 %shard_map.82 = f32[1024,256]{1,0:T(8,128)} custom-call(s32[8,16]{1,0:T(8,128)} %bitcast.8, f32[1024,512]{1,0:T(8,128)} %bitcast.7, f32[512,256]{1,0:T(8,128)} %w_first_ref.1, f32[1,1024]{1,0:T(1,128)} %bitcast.9, f32[8,16,128,128]{3,2,1,0:T(8,128)} %bitcast.5, f32[256,1024]{1,0:T(8,128)} %w_in_hbm.1, f32[256,1024]{1,0:T(8,128)} %w_rec_hbm.1, ...), custom_call_target="tpu_custom_call" | custom-call | tf_op jit(solution)/shard_map/pallas_call | solution.py:466
  227.6 2.3 copy.10

commit v3 on v2

--- a/solution.py
+++ b/solution.py
@@ -13,7 +13,9 @@
 LANES = 128
 KT = 16
 BLOCKS = 8
-BATCH = 32
+BATCHES = (16, 48)
+ROWS = 1024
+EARLY = SNAPS * BATCHES[0] // EDGE
 HIDDEN = 256
 GATHER_SEMS = 40
 
@@ -37,8 +39,8 @@
 
 
 class Gather:
-    def __init__(self, buffer, source, first, count, send_sem, recv_sem, base):
-        self.buffer, self.source, self.first, self.count = buffer, source, first, count
+    def __init__(self, buffer, first, count, send_sem, recv_sem, base):
+        self.buffer, self.first, self.count = buffer, first, count
         self.send_sem, self.recv_sem, self.base = send_sem, recv_sem, base
         me = lax.axis_index("vtx")
         self.x, self.y = lax.rem(me, SIDE), lax.div(me, SIDE)
@@ -49,17 +51,16 @@
         dx, dy = (da, db) if half == 0 else (db, da)
         return lax.rem(self.y + (dy + SIDE), SIDE) * SIDE + lax.rem(self.x + (dx + SIDE), SIDE)
 
-    def rows(self, half, part):
+    def place(self, half, da, db, part):
         size = self.count // 2
-        start = half * size
-        if part is not None:
-            size //= 2
-            start += part * size
-        return start, size
-
-    def place(self, half, da, db, part):
-        start, size = self.rows(half, part)
-        return self.buffer.at[pl.ds(self.device(half, da, db) * BLOCKS + (self.first + start), size)]
+        block = self.device(half, da, db) * BLOCKS + (self.first + half * size)
+        if part is None:
+            return self.buffer.at[pl.ds(block, size)]
+        if size == 1:
+            return self.buffer.at[pl.ds(block, 1), pl.ds(part * (EDGE // 2), EDGE // 2)]
+        longer_last = half == 1 if db == 0 else da in (-1, 1)
+        cut = size // 2 if longer_last else size - size // 2
+        return self.buffer.at[pl.ds(block + part * cut, size - cut if part else cut)]
 
     def number(self, half, da, db, part):
         along = {-1: 0, 1: 1, 2: 2}
@@ -77,12 +78,8 @@
         else:
             to, number = self.device(half, 0, way), self.number(half, da, seen(db), part)
         place = self.place(half, da, db, part)
-        source = place
-        if da == 0 and db == 0 and self.source is not None:
-            start, size = self.rows(half, part)
-            source = self.source.at[pl.ds(self.first + start, size)]
         return pltpu.make_async_remote_copy(
-            src_ref=source,
+            src_ref=place,
             dst_ref=place,
             send_sem=self.send_sem.at[number],
             recv_sem=self.recv_sem.at[number],
@@ -111,6 +108,11 @@
         for way in (1, -1):
             self.send(half, 1, way, da, 0)
 
+    def own_half(self, half):
+        for way in (1, -1):
+            self.send(half, 0, way, 0, 0)
+        self.both(half, 0)
+
     def own(self):
         for half in (0, 1):
             for way in (1, -1):
@@ -153,14 +155,15 @@
 
 
 def kernel(
-    ids_ref, feats_ref, w_first_ref, bias_ref, tiles_hbm, w_in_hbm, w_rec_hbm, w_two_hbm, out_ref,
-    buf0, buf1, staged, tcat, scales, ycat, hid, xin, pre, zout, zin,
-    w_in, w_rec, w_two, in_high, in_low, rec_high, rec_low,
-    g_send, g_recv, x_send, x_recv, z_send, z_recv, local_sem, tile_sem, weight_sem, free_sem,
+    ids_ref, bias_ref, feats_hbm, w_first_hbm, tiles_hbm, w_in_hbm, w_rec_hbm, w_two_hbm, out_ref,
+    buf0, buf1, staged, tcat, scales, ycat, hid, xin0, xin1, pre0, pre1, zout0, zout1, zin,
+    feats, w_first, w_in, w_rec, w_two, in_high, in_low, rec_high, rec_low,
+    g_send, g_recv, x_send, x_recv, z_send, z_recv, local_sem, tile_sem, feats_sem, weight_sem, free_sem,
 ):
     snap, me = lax.axis_index("snap"), lax.axis_index("vtx")
     x, y = lax.rem(me, SIDE), lax.div(me, SIDE)
-    bufs = (buf0, buf1)
+    bufs, xin, pre, zout = (buf0, buf1), (xin0, xin1), (pre0, pre1), (zout0, zout1)
+    firsts = (0, SNAPS * BATCHES[0])
     others = [lax.rem(snap + k, SNAPS) for k in range(1, SNAPS)]
     beside = [
         lax.rem(y + dy, SIDE) * SIDE + lax.rem(x + dx, SIDE)
@@ -171,38 +174,48 @@
         pltpu.make_async_copy(a, b, weight_sem.at[i])
         for i, (a, b) in enumerate(((w_in_hbm, w_in), (w_rec_hbm, w_rec), (w_two_hbm, w_two)))
     ]
+    first_copies = [
+        pltpu.make_async_copy(w_first_hbm.at[rows], w_first.at[rows], feats_sem.at[BLOCKS + i])
+        for i, rows in enumerate((slice(0, HIDDEN), slice(HIDDEN, 2 * HIDDEN)))
+    ]
+    feats_copies = [
+        pltpu.make_async_copy(feats_hbm.at[rows], feats.at[rows], feats_sem.at[r])
+        for r, rows in enumerate(slice(r * EDGE, (r + 1) * EDGE) for r in range(BLOCKS))
+    ]
 
     def tile_copy(r):
         return pltpu.make_async_copy(tiles_hbm.at[r], staged.at[r], tile_sem.at[r])
 
+    for copy in (*first_copies, *feats_copies):
+        copy.start()
     barrier = pltpu.get_barrier_semaphore()
     for device in beside:
         pl.semaphore_signal(barrier, inc=1, device_id={"vtx": device}, device_id_type=MESH)
     for device in others:
         pl.semaphore_signal(barrier, inc=1, device_id={"snap": device}, device_id_type=MESH)
 
+    one = [Gather(bufs[c], 0, BLOCKS, g_send, g_recv, c * GATHER_SEMS) for c in (0, 1)]
+    for copy in first_copies:
+        copy.wait()
+
+    def first_product(c, half):
+        high, low = halves(w_first[:, c * LANES : (c + 1) * LANES])
+        for r in range(4 * half, 4 * half + 4):
+            if c == 0:
+                feats_copies[r].wait()
+            bufs[c][me * BLOCKS + r] = dot3(feats[r * EDGE : (r + 1) * EDGE, :], high, low)
+
+    first_product(0, 0)
+    pl.semaphore_wait(barrier, len(beside) + len(others))
+    one[0].own_half(0)
+    first_product(0, 1)
+    one[0].own_half(1)
     for r in range(BLOCKS):
         tile_copy(r).start()
     for copy in weights:
         copy.start()
-
-    def first_product(c):
-        high, low = halves(w_first_ref[:, c * LANES : (c + 1) * LANES])
-
-        def some(i, _):
-            part = dot3(feats_ref[pl.ds(i * 256, 256), :], high, low)
-            bufs[c][me * BLOCKS + 2 * i] = part[:EDGE]
-            bufs[c][me * BLOCKS + 2 * i + 1] = part[EDGE:]
-            return 0
-
-        lax.fori_loop(0, BLOCKS // 2, some, 0)
-
-    first_product(0)
-    pl.semaphore_wait(barrier, len(beside) + len(others))
-
-    one = [Gather(bufs[c], None, 0, BLOCKS, g_send, g_recv, c * GATHER_SEMS) for c in (0, 1)]
-    one[0].own()
-    first_product(1)
+    first_product(1, 0)
+    first_product(1, 1)
 
     def split_tiles(start, stop):
         def block(r, _):
@@ -228,18 +241,18 @@
                 ycat[k * EDGE : (k + 1) * EDGE, LANES:] = low
             out = dot(tcat[r], ycat[...])
             total = (out[:EDGE, :LANES] + out[:EDGE, LANES:]) + (out[EDGE:, :LANES] + out[EDGE:, LANES:])
+            rows = pl.ds(pl.multiple_of(r * EDGE, EDGE), EDGE)
             total = scales[r] * (bufs[c][me * BLOCKS + r] + total)
             if first:
-                hid[c, r] = jnp.maximum(total, 0.0)
+                hid[c, rows] = jnp.maximum(total, 0.0)
             else:
-                out_ref[pl.ds(pl.multiple_of(r * EDGE, EDGE), EDGE), c * LANES : (c + 1) * LANES] = total
+                out_ref[rows, c * LANES : (c + 1) * LANES] = total
             return 0
 
         lax.fori_loop(start, stop, block, 0)
 
     def shares(ref, c, b, j):
-        rows = pl.ds(pl.multiple_of(lax.rem(j, 4) * BATCH, BATCH), BATCH)
-        return ref.at[c, 4 * b + lax.div(j, 4), rows]
+        return ref.at[c, pl.ds(pl.multiple_of(firsts[b] + j * BATCHES[b], 16), BATCHES[b])]
 
     x_sent = []
 
@@ -247,7 +260,7 @@
         to = others[k - 1]
         return pltpu.make_async_remote_copy(
             src_ref=shares(hid, c, b, to),
-            dst_ref=xin.at[c, b, snap],
+            dst_ref=xin[b].at[c, snap],
             send_sem=x_send.at[c, b, k],
             recv_sem=x_recv.at[c, b, k],
             device_id={"snap": to},
@@ -255,7 +268,7 @@
         )
 
     def x_local(c, b):
-        return pltpu.make_async_copy(shares(hid, c, b, snap), xin.at[c, b, snap], x_send.at[c, b, 0])
+        return pltpu.make_async_copy(shares(hid, c, b, snap), xin[b].at[c, snap], x_send.at[c, b, 0])
 
     def x_start(c, b):
         for k in range(1, SNAPS):
@@ -269,28 +282,30 @@
         for k in range(1, SNAPS):
             source = lax.rem(snap + (SNAPS - k), SNAPS)
             pltpu.make_async_remote_copy(
-                src_ref=xin.at[c, b, source],
-                dst_ref=xin.at[c, b, source],
+                src_ref=xin[b].at[c, source],
+                dst_ref=xin[b].at[c, source],
                 send_sem=x_send.at[c, b, k],
                 recv_sem=x_recv.at[c, b, k],
                 device_id={"snap": source},
                 device_id_type=MESH,
             ).wait_recv()
 
-    def input_product(c, b):
-        deep = slice(c * LANES, (c + 1) * LANES)
+    def input_product(b):
+        count = 256 // BATCHES[b] if b == 0 else 4
+        size = count * BATCHES[b]
 
         def some(i, _):
-            rows = pl.ds(pl.multiple_of(i * EDGE, EDGE), EDGE)
-            part = dot3(xin[c, b, pl.ds(i * 4, 4)].reshape(EDGE, LANES), in_high[deep, :], in_low[deep, :])
-            pre[b, rows] = part + (bias_ref[...] if c == 0 else pre[b, rows])
+            rows = pl.ds(pl.multiple_of(i * size, size), size)
+            steps = pl.ds(i * count, count)
+            both = [xin[b][c, steps].reshape(size, LANES) for c in (0, 1)]
+            pre[b][rows] = dot3(jnp.concatenate(both, axis=1), in_high[...], in_low[...]) + bias_ref[...]
             return 0
 
-        lax.fori_loop(0, SNAPS * BATCH // EDGE, some, 0)
+        lax.fori_loop(0, SNAPS // count, some, 0)
 
     def z_copy(b, s):
         return pltpu.make_async_remote_copy(
-            src_ref=zout.at[b, s],
+            src_ref=zout[b].at[s],
             dst_ref=shares(zin, slice(None), b, snap),
             send_sem=z_send.at[b, s],
             recv_sem=z_recv.at[b, snap],
@@ -299,11 +314,11 @@
         )
 
     def z_local(b):
-        return pltpu.make_async_copy(zout.at[b, snap], shares(zin, slice(None), b, snap), local_sem.at[b])
+        return pltpu.make_async_copy(zout[b].at[snap], shares(zin, slice(None), b, snap), local_sem.at[b])
 
     def z_start(b, s, z):
-        zout[b, s, 0] = z[:, :LANES]
-        zout[b, s, 1] = z[:, LANES:]
+        zout[b][s, 0] = z[:, :LANES]
+        zout[b][s, 1] = z[:, LANES:]
 
         @pl.when(s != snap)
         def _():
@@ -325,8 +340,9 @@
                 device_id_type=MESH,
             ).wait_recv()
         for c in (0, 1):
-            for i in range(4 * b, 4 * b + 4):
-                bufs[c][me * BLOCKS + i] = zin[c, i]
+            size = SNAPS * BATCHES[b]
+            own = pl.ds(me * BLOCKS + firsts[b] // EDGE, size // EDGE)
+            bufs[c][own] = zin[c, firsts[b] : firsts[b] + size].reshape(size // EDGE, EDGE, LANES)
 
     def cell(gates, state_c):
         i, f, g, o = (gates[:, q * HIDDEN : (q + 1) * HIDDEN] for q in range(4))
@@ -334,19 +350,20 @@
         return sigmoid(o) * jnp.tanh(state_c), state_c
 
     def begin(b):
-        return cell(pre[b, :BATCH], jnp.zeros((BATCH, HIDDEN), F32))
+        return cell(pre[b][: BATCHES[b]], jnp.zeros((BATCHES[b], HIDDEN), F32))
 
     def product(h):
         high, low = halves(h)
         both = dot(jnp.concatenate([high, low], axis=0), rec_high[...])
-        return both[:BATCH] + (both[BATCH:] + dot(high, rec_low[...]))
+        rows = h.shape[0]
+        return both[:rows] + (both[rows:] + dot(high, rec_low[...]))
 
     def steps(b, start, stop, carry):
         def advance(s, carry):
             h, state_c = carry
             wide = product(h)
-            rows = pl.ds(pl.multiple_of(s * BATCH, BATCH), BATCH)
-            new = cell(pre[b, rows] + wide[:, : 4 * HIDDEN], state_c)
+            rows = pl.ds(pl.multiple_of(s * BATCHES[b], 16), BATCHES[b])
+            new = cell(pre[b][rows] + wide[:, : 4 * HIDDEN], state_c)
             z_start(b, s - 1, wide[:, 4 * HIDDEN :])
             return new
 
@@ -366,81 +383,78 @@
     rec_high[:, 4 * HIDDEN :], rec_low[:, 4 * HIDDEN :] = halves(w_two[...])
     one[0].onward(0)
     one[0].opposite()
+    one[1].own()
     one[0].onward(-1)
     one[0].onward(1)
-    one[1].own()
+    one[1].ring()
     one[0].onward(2)
-    one[0].last()
-
-    conv(0, 0, 4, True)
-    x_start(0, 0)
-    one[1].ring()
-    conv(0, 4, 8, True)
-    x_start(0, 1)
     one[1].onward(0)
     one[1].opposite()
+    one[0].last()
+
+    conv(0, 0, EARLY, True)
+    x_start(0, 0)
+    one[1].onward(-1)
+    one[1].onward(1)
+    conv(0, EARLY, BLOCKS, True)
+    x_start(0, 1)
+    one[1].onward(2)
     x_wait(0, 0)
     x_wait(0, 1)
-    input_product(0, 0)
-    one[1].onward(-1)
-    one[1].onward(1)
-    input_product(0, 1)
-    one[1].onward(2)
     one[1].last()
 
-    conv(1, 0, 4, True)
+    conv(1, 0, EARLY, True)
     x_start(1, 0)
-    conv(1, 4, 8, True)
+    conv(1, EARLY, BLOCKS, True)
     x_start(1, 1)
+
+    x_wait(1, 0)
+    input_product(0)
+    finish(0, steps(0, 1, SNAPS, begin(0)))
     one[0].wait_sent()
     one[1].wait_sent()
     for device in beside:
         pl.semaphore_signal(free_sem, inc=1, device_id={"vtx": device}, device_id_type=MESH)
-
-    x_wait(1, 0)
-    input_product(1, 0)
-    finish(0, steps(0, 1, SNAPS, begin(0)))
     x_wait(1, 1)
-    input_product(1, 1)
-    carry = steps(1, 1, 8, begin(1))
+    input_product(1)
     z_wait(0)
     pl.semaphore_wait(free_sem, len(beside))
     two = [
         [
-            Gather(bufs[c], zin.at[c], 4 * b, 4, g_send, g_recv, (2 + 2 * b + c) * GATHER_SEMS)
+            Gather(bufs[c], first, count, g_send, g_recv, (2 + 2 * b + c) * GATHER_SEMS)
             for c in (0, 1)
         ]
-        for b in (0, 1)
+        for b, (first, count) in enumerate(((0, EARLY), (EARLY, BLOCKS - EARLY)))
     ]
     two[0][0].own()
     two[0][1].own()
-    finish(1, steps(1, 8, SNAPS, carry))
+    carry = steps(1, 1, 8, begin(1))
     two[0][0].ring()
     two[0][1].ring()
-    z_wait(1)
-    two[1][0].own()
+    finish(1, steps(1, 8, SNAPS, carry))
     two[0][0].onward(0)
     two[0][0].opposite()
     two[0][1].onward(0)
     two[0][1].opposite()
     for da in (-1, 1, 2):
         two[0][0].onward(da)
+        two[0][1].onward(da)
+    z_wait(1)
+    two[1][0].own()
     two[1][1].own()
+    two[0][0].last()
+    two[0][1].last()
     two[1][0].ring()
-    for da in (-1, 1, 2):
-        two[0][1].onward(da)
     two[1][0].onward(0)
     two[1][0].opposite()
     two[1][1].ring()
-    for da in (-1, 1, 2):
-        two[1][0].onward(da)
-    two[0][0].last()
-    two[0][1].last()
-    two[1][0].last()
-    conv(0, 0, 2, False)
+    two[1][0].onward(-1)
+    two[1][0].onward(1)
     two[1][1].onward(0)
     two[1][1].opposite()
-    conv(0, 2, 4, False)
+    two[1][0].onward(2)
+    two[1][0].last()
+    conv(0, 0, 4, False)
     two[1][1].onward(-1)
     two[1][1].onward(1)
     conv(0, 4, 8, False)
@@ -459,27 +473,28 @@
 
 
 def on_device(feats, col_ids, tiles, w_first, w_input, w_recur, lstm_bias, w_second):
-    rows = BLOCKS * EDGE
-    whole = (lax.axis_size("vtx") * BLOCKS, EDGE, LANES)
+    everyone = (lax.axis_size("vtx") * BLOCKS, EDGE, LANES)
     vmem, hbm = pl.BlockSpec(memory_space=pltpu.VMEM), pl.BlockSpec(memory_space=pl.ANY)
     dma = pltpu.SemaphoreType.DMA
     out = pl.pallas_call(
         kernel,
-        in_specs=[pl.BlockSpec(memory_space=pltpu.SMEM), vmem, vmem, vmem, hbm, hbm, hbm, hbm],
+        in_specs=[pl.BlockSpec(memory_space=pltpu.SMEM), vmem, *[hbm] * 6],
         out_specs=vmem,
-        out_shape=jax.ShapeDtypeStruct((rows, HIDDEN), F32),
+        out_shape=pltpu.VMEM((ROWS, HIDDEN), F32),
         scratch_shapes=[
-            pltpu.VMEM(whole, F32),
-            pltpu.VMEM(whole, F32),
+            pltpu.VMEM(everyone, F32),
+            pltpu.VMEM(everyone, F32),
             pltpu.VMEM((BLOCKS, KT, EDGE, EDGE), F32),
             pltpu.VMEM((BLOCKS, 2 * EDGE, KT * EDGE), BF16),
             pltpu.VMEM((BLOCKS, EDGE, LANES), F32),
             pltpu.VMEM((KT * EDGE, 2 * LANES), BF16),
-            pltpu.VMEM((2, BLOCKS, EDGE, LANES), F32),
-            pltpu.VMEM((2, 2, SNAPS, BATCH, LANES), F32),
-            pltpu.VMEM((2, SNAPS * BATCH, 4 * HIDDEN), F32),
-            pltpu.VMEM((2, SNAPS, 2, BATCH, LANES), F32),
-            pltpu.VMEM((2, BLOCKS, EDGE, LANES), F32),
+            pltpu.VMEM((2, ROWS, LANES), F32),
+            *[pltpu.VMEM((2, SNAPS, batch, LANES), F32) for batch in BATCHES],
+            *[pltpu.VMEM((SNAPS * batch, 4 * HIDDEN), F32) for batch in BATCHES],
+            *[pltpu.VMEM((SNAPS, 2, batch, LANES), F32) for batch in BATCHES],
+            pltpu.VMEM((2, ROWS, LANES), F32),
+            pltpu.VMEM(feats.shape[1:], F32),
+            pltpu.VMEM(w_first.shape, F32),
             pltpu.VMEM((HIDDEN, 4 * HIDDEN), F32),
             pltpu.VMEM((HIDDEN, 4 * HIDDEN), F32),
             pltpu.VMEM((HIDDEN, HIDDEN), F32),
@@ -495,14 +510,15 @@
             dma((2, SNAPS)),
             dma((2,)),
             dma((BLOCKS,)),
+            dma((BLOCKS + 2,)),
             dma((3,)),
             pltpu.SemaphoreType.REGULAR,
         ],
         compiler_params=pltpu.CompilerParams(
-            collective_id=0, has_side_effects=True, vmem_limit_bytes=58 << 20
+            collective_id=0, has_side_effects=True, vmem_limit_bytes=56 << 20
         ),
     )(
-        col_ids[0], feats[0], w_first, lstm_bias.reshape(1, -1), tiles[0], w_input, w_recur, w_second
+        col_ids[0], lstm_bias.reshape(1, -1), feats[0], w_first, tiles[0], w_input, w_recur, w_second
     )
     return out[None]
 

time: 233 us -> 225 us (0.966)
  Pallas kernels: 228 us -> 221 us
    pallas_call x1, Pallas kernels: 228 us -> 221 us  [on_device(): pl.pallas_call(kernel, in_specs=[pl.BlockSpec(memory_space=pltpu.SMEM), v...]
where the time goes in v3:
time: 225 us; the launch traced here: 222 us
  Pallas kernels  221 us (98%)
    pallas_call x1, Pallas kernels, on_device(): pl.pallas_call(kernel, in_specs=[pl.BlockSpec(memory_space=pltpu.SMEM), v...  221 us

profile of v3, /device:TPU:1, one launch (start us, length us, event | category | flops | bytes accessed | tf_op | source)
XLA Modules:
  0.0 222.2 jit_solution(5164912100890262744)
XLA Ops:
  0.0 221.2 %shard_map.82 = f32[1024,256]{1,0:T(8,128)S(1)} custom-call(s32[8,16]{1,0:T(8,128)} %bitcast.8, f32[1,1024]{1,0:T(1,128)} %bitcast.9, f32[1024,512]{1,0:T(8,128)} %bitcast.7, f32[512,256]{1,0:T(8,128)} %w_first_hbm.1, f32[8,16,128,128]{3,2,1,0:T(8,128)} %bitcast.6, f32[256,1024]{1,0:T(8,128)} %w_in_hbm.1, f32[256,1024]{1,0:T(8,128)} %w_rec_hbm.1, ...), custom_call_target="tpu_custom_call" | custom-call | tf_op jit(solution)/shard_map/pallas_call | solution.py:479
  221.2 1.0 copy.10

commit v4 on v3

--- a/solution.py
+++ b/solution.py
@@ -56,11 +56,7 @@
         block = self.device(half, da, db) * BLOCKS + (self.first + half * size)
         if part is None:
             return self.buffer.at[pl.ds(block, size)]
-        if size == 1:
-            return self.buffer.at[pl.ds(block, 1), pl.ds(part * (EDGE // 2), EDGE // 2)]
-        longer_last = half == 1 if db == 0 else da in (-1, 1)
-        cut = size // 2 if longer_last else size - size // 2
-        return self.buffer.at[pl.ds(block + part * cut, size - cut if part else cut)]
+        return self.buffer.at[pl.ds(block, size), pl.ds(part * (EDGE // 2), EDGE // 2)]
 
     def number(self, half, da, db, part):
         along = {-1: 0, 1: 1, 2: 2}
@@ -394,9 +390,10 @@
 
     conv(0, 0, EARLY, True)
     x_start(0, 0)
+    conv(0, EARLY, 4, True)
     one[1].onward(-1)
     one[1].onward(1)
-    conv(0, EARLY, BLOCKS, True)
+    conv(0, 4, BLOCKS, True)
     x_start(0, 1)
     one[1].onward(2)
     x_wait(0, 0)
@@ -428,10 +425,9 @@
     ]
     two[0][0].own()
     two[0][1].own()
-    carry = steps(1, 1, 8, begin(1))
+    finish(1, steps(1, 1, SNAPS, begin(1)))
     two[0][0].ring()
     two[0][1].ring()
-    finish(1, steps(1, 8, SNAPS, carry))
     two[0][0].onward(0)
     two[0][0].opposite()
     two[0][1].onward(0)

time: 225 us -> 221 us (0.982); the launches traced: 222 us -> 221 us
  no operation moved by 1% of the time
where the time goes in v4:
time: 221 us
  Pallas kernels  220 us (100%)
    pallas_call x1, Pallas kernels, on_device(): pl.pallas_call(kernel, in_specs=[pl.BlockSpec(memory_space=pltpu.SMEM), v...  220 us

profile of v4, /device:TPU:1, one launch (start us, length us, event | category | flops | bytes accessed | tf_op | source)
XLA Modules:
  0.0 221.2 jit_solution(8557995372363928972)
XLA Ops:
  0.0 220.2 %shard_map.82 = f32[1024,256]{1,0:T(8,128)S(1)} custom-call(s32[8,16]{1,0:T(8,128)} %bitcast.8, f32[1,1024]{1,0:T(1,128)} %bitcast.9, f32[1024,512]{1,0:T(8,128)} %bitcast.7, f32[512,256]{1,0:T(8,128)} %w_first_hbm.1, f32[8,16,128,128]{3,2,1,0:T(8,128)} %bitcast.6, f32[256,1024]{1,0:T(8,128)} %w_in_hbm.1, f32[256,1024]{1,0:T(8,128)} %w_rec_hbm.1, ...), custom_call_target="tpu_custom_call" | custom-call | tf_op jit(solution)/shard_map/pallas_call | solution.py:475
  220.2 1.0 copy.10

commit v5 on v4

--- a/solution.py
+++ b/solution.py
@@ -230,12 +230,12 @@
         lax.fori_loop(start, stop, block, 0)
 
     def conv(c, start, stop, first):
-        def block(r, _):
+        def one_block(r, slot):
             for k in range(KT):
                 high, low = halves(bufs[c][ids_ref[r, k]])
-                ycat[k * EDGE : (k + 1) * EDGE, :LANES] = high
-                ycat[k * EDGE : (k + 1) * EDGE, LANES:] = low
-            out = dot(tcat[r], ycat[...])
+                ycat[slot, k * EDGE : (k + 1) * EDGE, :LANES] = high
+                ycat[slot, k * EDGE : (k + 1) * EDGE, LANES:] = low
+            out = dot(tcat[r], ycat[slot])
             total = (out[:EDGE, :LANES] + out[:EDGE, LANES:]) + (out[EDGE:, :LANES] + out[EDGE:, LANES:])
             rows = pl.ds(pl.multiple_of(r * EDGE, EDGE), EDGE)
             total = scales[r] * (bufs[c][me * BLOCKS + r] + total)
@@ -243,9 +243,13 @@
                 hid[c, rows] = jnp.maximum(total, 0.0)
             else:
                 out_ref[rows, c * LANES : (c + 1) * LANES] = total
+
+        def pair(i, _):
+            for slot in (0, 1):
+                one_block(start + 2 * i + slot, slot)
             return 0
 
-        lax.fori_loop(start, stop, block, 0)
+        lax.fori_loop(0, (stop - start) // 2, pair, 0)
 
     def shares(ref, c, b, j):
         return ref.at[c, pl.ds(pl.multiple_of(firsts[b] + j * BATCHES[b], 16), BATCHES[b])]
@@ -483,7 +487,7 @@
             pltpu.VMEM((BLOCKS, KT, EDGE, EDGE), F32),
             pltpu.VMEM((BLOCKS, 2 * EDGE, KT * EDGE), BF16),
             pltpu.VMEM((BLOCKS, EDGE, LANES), F32),
-            pltpu.VMEM((KT * EDGE, 2 * LANES), BF16),
+            pltpu.VMEM((2, KT * EDGE, 2 * LANES), BF16),
             pltpu.VMEM((2, ROWS, LANES), F32),
             *[pltpu.VMEM((2, SNAPS, batch, LANES), F32) for batch in BATCHES],
             *[pltpu.VMEM((SNAPS * batch, 4 * HIDDEN), F32) for batch in BATCHES],

time: 221 us -> 220 us (level)
    pallas_call x1, Pallas kernels: 220 us -> 218 us  [on_device(): pl.pallas_call(kernel, in_specs=[pl.BlockSpec(memory_space=pltpu.SMEM), v...]
where the time goes in v5:
time: 220 us; the launch traced here: 219 us
  Pallas kernels  218 us (99%)
    pallas_call x1, Pallas kernels, on_device(): pl.pallas_call(kernel, in_specs=[pl.BlockSpec(memory_space=pltpu.SMEM), v...  218 us

profile of v5, /device:TPU:1, one launch (start us, length us, event | category | flops | bytes accessed | tf_op | source)
XLA Modules:
  0.0 218.9 jit_solution(108242572010976216)
XLA Ops:
  0.0 217.9 %shard_map.82 = f32[1024,256]{1,0:T(8,128)S(1)} custom-call(s32[8,16]{1,0:T(8,128)} %bitcast.8, f32[1,1024]{1,0:T(1,128)} %bitcast.9, f32[1024,512]{1,0:T(8,128)} %bitcast.7, f32[512,256]{1,0:T(8,128)} %w_first_hbm.1, f32[8,16,128,128]{3,2,1,0:T(8,128)} %bitcast.6, f32[256,1024]{1,0:T(8,128)} %w_in_hbm.1, f32[256,1024]{1,0:T(8,128)} %w_rec_hbm.1, ...), custom_call_target="tpu_custom_call" | custom-call | tf_op jit(solution)/shard_map/pallas_call | solution.py:479
  217.9 1.0 copy.10
